TPU v7x, 128 devices: a whole 4x4x4 slice. The times are simulated.
128 devices in a mesh: pipe: 4 (over x), dp: 4 (over y_hi, core), tensor: 8 (over z, y_lo).
Axes of the slice: x: 4, y: 4 (y_hi: 2, y_lo: 2; y = y_hi * 2 + y_lo), z: 4, core: 2. Of those that a mesh axis runs over, the one named last changes fastest.
Arguments:
- activations: bfloat16 [4, 4, 1024, 8192], P('pipe', 'dp', None, 'tensor'), may hold values from -6 to 6
- analysis: bfloat16 [4, 8192, 2048], P('pipe', 'tensor'), may hold values from -0.0625 to 0.0625
- synthesis: bfloat16 [4, 2048, 8192], P('pipe', None, 'tensor'), may hold values from -0.125 to 0.125
- norm_gain: float32 [4, 8192], P('pipe'), may hold values from 0.1 to 1.9
- query_weight: bfloat16 [4, 8192, 4096], P('pipe', None, 'tensor'), may hold values from -4 to 4
- keys_values: bfloat16 [4, 8192, 2048], P('pipe', None, 'tensor'), may hold values from -1 to 1
- latent_grad: bfloat16 [4, 4, 1024, 2048], P('pipe', 'dp', 'tensor'), may hold values from -6 to 6
Outputs:
- attended: bfloat16 [4, 4, 1024, 4096], P('pipe', 'dp', None, 'tensor')
- activation_grad: bfloat16 [4, 4, 1024, 8192], P('pipe', 'dp', None, 'tensor')
All inputs are finite; a program needn't handle non-finite values.
Results may differ from a plain program's by a relative error of at most 0.017.
Values may be sent and summed in bfloat16 or wider, within the bound.
A program may use at most 192 MiB of HBM per device.

v0:
```python
import jax
import jax.numpy as jnp
from jax import lax
from jax.sharding import PartitionSpec as P

D = 8192
HEAD = 128


EPSILON = 1e-05
ROPE_BASE = 500000.0


def passed_along(value, axis, steps):
    count = lax.axis_size(axis)
    pairs = [(source, (source + steps) % count) for source in range(count)]
    return lax.ppermute(value, axis, pairs)


def rotary(inputs, positions):
    half_width = inputs.shape[-1] // 2
    frequency = ROPE_BASE ** (-(jnp.arange(half_width, dtype=jnp.float32) * 2.0 / inputs.shape[-1]))
    angles = positions[:, None] * frequency[None, :]
    cosine = jnp.cos(angles)[:, None, :]
    sine_table = jnp.sin(angles)[:, None, :]
    leading = inputs[..., :half_width]
    trailing = inputs[..., half_width:]
    return jnp.concatenate(
        [leading * cosine - trailing * sine_table, trailing * cosine + leading * sine_table],
        axis=-1,
    )


def attend(queries, rotated_keys, values_in, anchor):
    row_count = queries.shape[0]
    scores = jnp.einsum(
        "qkgd,skd->kgqs", queries, rotated_keys, preferred_element_type=jnp.float32
    ) * HEAD ** (-0.5)
    row_pos = anchor + jnp.arange(row_count, dtype=jnp.int32)
    col_pos = jnp.arange(rotated_keys.shape[0], dtype=jnp.int32)
    visible = col_pos[None, :] <= row_pos[:, None]
    scores = jnp.where(visible[None, None], scores, -1e30)
    maximum = jnp.max(scores, axis=-1, keepdims=True)
    exponent = jnp.exp(scores - maximum)
    weights = (exponent / jnp.sum(exponent, axis=-1, keepdims=True)).astype(jnp.bfloat16)
    mixed_values = jnp.einsum(
        "kgqs,skd->qkgd", weights, values_in, preferred_element_type=jnp.float32
    )
    return mixed_values.astype(jnp.bfloat16).reshape(row_count, -1)


def on_device(activations, analysis, synthesis, norm_gain, query_weight, keys_values, latent_grad):
    acts_local = activations[0, 0]
    w_analysis = analysis[0]
    w_synth = synthesis[0]
    gain_all = norm_gain[0]
    w_query = query_weight[0]
    w_keyval = keys_values[0]
    length = acts_local.shape[0]
    width_local = w_synth.shape[1]
    latent_own = lax.psum_scatter(
        jnp.dot(acts_local, w_analysis, preferred_element_type=jnp.float32),
        "tensor",
        scatter_dimension=0,
        tiled=True,
    ).astype(jnp.bfloat16)
    arrived = passed_along(latent_own, "pipe", 1)
    latent_full = lax.all_gather(arrived, "tensor", axis=0, tiled=True)
    synthesized = jnp.dot(latent_full, w_synth, preferred_element_type=jnp.float32).astype(
        jnp.bfloat16
    )
    synth_float = synthesized.astype(jnp.float32)
    squares = lax.psum(jnp.sum(synth_float * synth_float, axis=1), "tensor")
    offset = lax.axis_index("tensor") * width_local
    gain_own = lax.dynamic_slice_in_dim(gain_all, offset, width_local, 0)
    normed = (synth_float * lax.rsqrt(squares / D + EPSILON)[:, None] * gain_own[None, :]).astype(
        jnp.bfloat16
    )
    portion = lax.all_gather(normed, "tensor", axis=1, tiled=True)
    queries_all = jnp.dot(portion, w_query, preferred_element_type=jnp.float32)
    keyvals_all = jnp.dot(portion, w_keyval, preferred_element_type=jnp.float32)
    heads_query = w_query.shape[1] // HEAD
    heads_keyval = w_keyval.shape[1] // (2 * HEAD)
    per_group = heads_query // heads_keyval
    positions = jnp.arange(length, dtype=jnp.float32)
    queries = rotary(queries_all.reshape(length, heads_query, HEAD), positions).astype(jnp.bfloat16)
    queries = queries.reshape(length, heads_keyval, per_group, HEAD)
    key_value = keyvals_all.reshape(length, heads_keyval, 2, HEAD)
    rotated_keys = rotary(key_value[:, :, 0], positions).astype(jnp.bfloat16)
    values_in = key_value[:, :, 1].astype(jnp.bfloat16)
    block_rows = min(512, length)
    outputs = []
    for block_index in range(length // block_rows):
        anchor = block_index * block_rows
        finish = anchor + block_rows
        outputs.append(
            attend(queries[anchor:finish], rotated_keys[:finish], values_in[:finish], anchor)
        )
    attended = jnp.concatenate(outputs, axis=0)
    returned = passed_along(latent_grad[0, 0], "pipe", -1)
    grad_local = lax.dot_general(
        lax.all_gather(returned, "tensor", axis=0, tiled=True),
        w_analysis,
        (((1,), (1,)), ((), ())),
        preferred_element_type=jnp.float32,
    ).astype(jnp.bfloat16)
    return (attended[None, None], grad_local[None, None])


def solution(mesh):
    return jax.shard_map(
        on_device,
        mesh=mesh,
        in_specs=(
            P("pipe", "dp", None, "tensor"),
            P("pipe", "tensor", None),
            P("pipe", None, "tensor"),
            P("pipe", None),
            P("pipe", None, "tensor"),
            P("pipe", None, "tensor"),
            P("pipe", "dp", "tensor", None),
        ),
        out_specs=(P("pipe", "dp", None, "tensor"), P("pipe", "dp", None, "tensor")),
        check_vma=False,
    )
```

profile of v0, /device:TPU:6, one launch (start us, length us, event | category | flops | bytes accessed | tf_op | source)
XLA Modules:
  0.0 763.5 jit_solution(12320643872794407464)
XLA Ops:
  7.2 0.0 copy-start
  7.2 0.0 reduce-scatter.2.cloned.1.call-start
  7.2 1.5 copy-done
  8.8 8.8 %fusion.15 = f32[1024,2048]{1,0:T(8,128)} fusion(bf16[1,1024,2048]{2,1,0:T(8,128)(2,1)} %param.8, bf16[1,1,1024,1024]{3,2,1,0:T(8,128)(2,1)S(1)} %copy-done), kind=kOutput, calls=%fused_computation.21 | convolution fusion | flops 4294967296 | bytes 14680064 | tf_op jit(solution)/shard_map/dot_general | solution.py:62
  17.6 0.0 reduce-scatter.2.cloned.1.call-update
  17.6 0.0 all-gather.4.cloned.1.call-start
  17.7 171.6 %reduce-scatter.2.cloned.1.call-done = f32[128,2048]{1,0:T(8,128)} async-done(((f32[1024,2048]{1,0:T(8,128)}), f32[128,2048]{1,0:T(8,128)}) %reduce-scatter.2.cloned.1.call-update) | async-done | bytes 1048592 | tf_op jit(solution)/shard_map/reduce_scatter | solution.py:61
  189.3 1.3 convert_element_type.66
  190.5 0.6 collective-permute-start
  191.1 13.2 %collective-permute-done = bf16[128,2048]{1,0:T(8,128)(2,1)S(1)} collective-permute-done((bf16[128,2048]{1,0:T(8,128)(2,1)S(1)}, bf16[128,2048]{1,0:T(8,128)(2,1)S(1)}, u32[]{:S(2)}, u32[]{:S(2)}) %collective-permute-start) | collective-permute-done | bytes 524320 | tf_op jit(solution)/shard_map/ppermute | solution.py:17
  204.3 0.8 copy-done.9
  205.1 0.0 all-gather.4.cloned.1.call-update
  205.1 0.0 all-gather.8.cloned.1.call-start
  205.2 0.9 collective-permute-start.1
  206.1 13.2 %collective-permute-done.1 = bf16[128,2048]{1,0:T(8,128)(2,1)S(1)} collective-permute-done((bf16[128,2048]{1,0:T(8,128)(2,1)S(1)}, bf16[128,2048]{1,0:T(8,128)(2,1)S(1)}, u32[]{:S(2)}, u32[]{:S(2)}) %collective-permute-start.1) | collective-permute-done | bytes 524320 | tf_op jit(solution)/shard_map/ppermute | solution.py:17
  219.3 0.8 copy-done.8
  220.1 0.0 all-gather.8.cloned.1.call-update
  220.1 0.0 all-gather.6.cloned.1.call-start
  220.2 0.7 constant_dynamic-slice_fusion
  220.9 76.4 %all-gather.4.cloned.1.call-done = bf16[1024,2048]{1,0:T(8,128)(2,1)} async-done(((bf16[128,2048]{1,0:T(8,128)(2,1)}), bf16[1024,2048]{1,0:T(8,128)(2,1)}) %all-gather.4.cloned.1.call-update) | async-done | bytes 4194320 | tf_op jit(solution)/shard_map/all_gather | solution.py:68
  297.3 8.1 %fusion.6 = (f32[1024]{0:T(1024)S(1)}, bf16[1024,1024]{0,1:T(8,128)(2,1)S(1)}) fusion(bf16[1024,2048]{1,0:T(8,128)(2,1)} %all-gather.4.cloned.1.call-done, bf16[1,2048,1024]{2,1,0:T(8,128)(2,1)} %param.9), kind=kOutput, calls=%fused_computation.11 | convolution fusion | flops 4299160576 | bytes 10489856 | tf_op jit(solution)/shard_map/dot_general | solution.py:69
  305.3 17.9 %psum.7 = f32[1024]{0:T(1024)S(1)} all-reduce(f32[1024]{0:T(1024)S(1)} %get-tuple-element.8), channel_id=1, replica_groups=mesh['pipe'=4,'dp'=4,'tensor'=8] {'tensor'}, use_global_device_ids=true, to_apply=%region_2.0 | all-reduce | flops 1024 | bytes 8192 | tf_op jit(solution)/shard_map/psum | solution.py:73
  323.2 1.8 fusion.8
  325.1 0.0 all-gather.6.cloned.1.call-update
  325.1 11.9 %copy.33 = bf16[512,8192]{1,0:T(8,128)(2,1)} copy(bf16[512,8192]{0,1:T(8,128)(2,1)} %bitcast.121) | data formatting | bytes 16777216 | tf_op jit(solution)/shard_map/dot_general | solution.py:80
  337.0 6.4 copy.30
  343.4 0.1 iota_compare_fusion.1
  343.4 1.0 fusion.46
  344.4 0.4 iota_compare_fusion
  344.8 45.9 %all-gather.8.cloned.1.call-done = bf16[1024,2048]{1,0:T(8,128)(2,1)} async-done(((bf16[128,2048]{1,0:T(8,128)(2,1)}), bf16[1024,2048]{1,0:T(8,128)(2,1)}) %all-gather.8.cloned.1.call-update) | async-done | bytes 4194320 | tf_op jit(solution)/shard_map/all_gather | solution.py:102
  390.7 9.3 %convert_bitcast_fusion = bf16[1,1,1024,1024]{3,2,1,0:T(8,128)(2,1)} fusion(bf16[1024,2048]{1,0:T(8,128)(2,1)} %all-gather.8.cloned.1.call-done, bf16[1,1024,2048]{2,1,0:T(8,128)(2,1)} %param.8), kind=kOutput, calls=%fused_computation.30 | convolution fusion | flops 4296015872 | bytes 10485760 | tf_op jit(solution)/shard_map/dot_general | solution.py:101
  400.0 317.7 %all-gather.6.cloned.1.call-done = bf16[1024,8192]{0,1:T(8,128)(2,1)} async-done(((bf16[1024,1024]{0,1:T(8,128)(2,1)}), bf16[1024,8192]{0,1:T(8,128)(2,1)}) %all-gather.6.cloned.1.call-update) | async-done | bytes 16777232 | tf_op jit(solution)/shard_map/all_gather | solution.py:79
  717.8 9.4 %fusion.28 = f32[1024,1,2,128]{0,3,2,1:T(8,128)S(1)} fusion(bf16[2,128,8192]{2,1,0:T(8,128)(2,1)} %bitcast.124, bf16[1024,8192]{0,1:T(8,128)(2,1)} %all-gather.6.cloned.1.call-done), kind=kOutput, calls=%fused_computation.34 | convolution fusion | flops 4294967296 | bytes 22020096 | tf_op jit(solution)/shard_map/dot_general | solution.py:81
  727.1 0.0 copy-start.2
  727.2 1.2 subtract_convert_fusion.1
  728.4 14.5 %fusion = f32[1024,4,128]{0,2,1:T(8,128)S(1)} fusion(bf16[4,128,8192]{2,1,0:T(8,128)(2,1)} %bitcast.122, bf16[1024,8192]{0,1:T(8,128)(2,1)} %all-gather.6.cloned.1.call-done), kind=kOutput, calls=%fused_computation | convolution fusion | flops 8589934592 | bytes 27262976 | tf_op jit(solution)/shard_map/dot_general | solution.py:80
  743.0 0.3 subtract_convert_fusion
  743.3 0.8 copy-done.4
  744.1 0.9 fusion.18
  745.1 0.9 fusion.17
  746.0 1.5 fusion.34
  747.5 0.2 copy.19
  747.7 1.6 fusion.5
  749.4 0.0 copy-start.3
  749.4 1.8 fusion.4
  751.3 3.4 fusion.31
  754.7 1.3 copy.20
  755.9 1.0 maximum_bitcast_fusion
  (24 shorter events, 0.1 us)
Async XLA Ops:
  7.2 1.6 copy-start
  7.2 182.1 %reduce-scatter.2.cloned.1.call-start = ((), (), s32[]{:S(2)}) async-start(), calls=%async_computation.1 | async-start | bytes 9437184 | tf_op jit(solution)/shard_map/reduce_scatter | solution.py:61
  17.6 187.6 %copy-start.12 = (bf16[1,1,128,2048]{3,2,1,0:T(8,128)(2,1)S(1)}, bf16[1,1,128,2048]{3,2,1,0:T(8,128)(2,1)}, u32[]{:S(2)}) copy-start(bf16[1,1,128,2048]{3,2,1,0:T(8,128)(2,1)} %param.13) | copy-start | bytes 1572868
  17.6 279.7 %all-gather.4.cloned.1.call-start = ((), (), s32[]{:S(2)}) async-start(), calls=%async_computation.2 | async-start | bytes 4718592 | tf_op jit(solution)/shard_map/all_gather | solution.py:68
  190.5 13.8 %collective-permute-start = (bf16[128,2048]{1,0:T(8,128)(2,1)S(1)}, bf16[128,2048]{1,0:T(8,128)(2,1)S(1)}, u32[]{:S(2)}, u32[]{:S(2)}) collective-permute-start(bf16[128,2048]{1,0:T(8,128)(2,1)S(1)} %convert_element_type.66), channel_id=1, source_target_pairs={{0,32},{32,64},{64,96},{96,0},{1,33},{33,65},{65,97},{97,1},{2,34}... | collective-permute-start | bytes 1572872 | tf_op jit(solution)/shard_map/ppermute | solution.py:17
  204.3 0.8 copy-start.9
  205.1 185.6 %all-gather.8.cloned.1.call-start = ((), (), s32[]{:S(2)}) async-start(), calls=%async_computation.4 | async-start | bytes 4718592 | tf_op jit(solution)/shard_map/all_gather | solution.py:102
  205.2 14.1 %collective-permute-start.1 = (bf16[128,2048]{1,0:T(8,128)(2,1)S(1)}, bf16[128,2048]{1,0:T(8,128)(2,1)S(1)}, u32[]{:S(2)}, u32[]{:S(2)}) collective-permute-start(bf16[128,2048]{1,0:T(8,128)(2,1)S(1)} %bitcast.130), channel_id=1, source_target_pairs={{0,96},{32,0},{64,32},{96,64},{1,97},{33,1},{65,33},{97,65},{2,98}... | collective-permute-start | bytes 1572872 | tf_op jit(solution)/shard_map/ppermute | solution.py:17
  219.3 0.8 copy-start.8
  220.1 497.7 %all-gather.6.cloned.1.call-start = ((), (), s32[]{:S(2)}) async-start(), calls=%async_computation.3 | async-start | bytes 18874368 | tf_op jit(solution)/shard_map/all_gather | solution.py:79
  727.1 1.3 copy-start.2
  728.4 14.9 %copy-start.10 = (bf16[1024,1,64]{0,2,1:T(8,128)(2,1)}, bf16[1024,1,64]{0,2,1:T(8,128)(2,1)S(1)}, u32[]{:S(2)}) copy-start(bf16[1024,1,64]{0,2,1:T(8,128)(2,1)S(1)} %get-tuple-element.5) | copy-start | bytes 393220
  743.3 0.8 copy-start.4
  743.3 1.7 copy-start.6
  746.0 1.7 copy-start.5
  746.0 1.7 copy-start.7
  746.0 1.7 copy-start.11
  749.4 1.9 copy-start.3
  751.3 5.7 copy-start.1
Sparse Core Ops, SparseCore 0:
  17.7 171.4 reduce-scatter.1
  205.2 91.9 all-gather.3
  299.5 91.1 all-gather.7
  392.2 325.4 all-gather.5
where the time goes:
time: 765 us; the launch traced here: 764 us
  waiting for transfers between devices  638 us (83%)
  matrix products  57.5 us (8%)
  local copies, waits for them, and re-layouts  24.4 us (3%)
  blocking collectives  17.9 us (2%)
  between operations  14 us (2%)
  other arithmetic  9.92 us (1%)
    all_gather x1, waiting for transfers between devices, on_device(): portion = lax.all_gather(normed, 'tensor', axis=1, tiled=True)  318 us
    reduce_scatter x1, waiting for transfers between devices, on_device(): lax.psum_scatter(jnp.dot(acts_local, w_analysis, preferred_element_type=j...  172 us
    all_gather x1, waiting for transfers between devices, on_device(): latent_full = lax.all_gather(arrived, 'tensor', axis=0, tiled=True)  76.4 us
    all_gather x1, waiting for transfers between devices, on_device(): lax.all_gather(returned, 'tensor', axis=0, tiled=True)  45.9 us
    ppermute x2, waiting for transfers between devices, passed_along(): return lax.ppermute(value, axis, pairs)  26.3 us
    psum x1, blocking collectives, on_device(): squares = lax.psum(jnp.sum(synth_float * synth_float, axis=1), 'tensor')  17.9 us
  transfers between devices with their start and end apart: 6, of which 6 were waited for; matrix products, arithmetic and copies ran while one was open for 5% of the time, Pallas kernels for 0%

commit v1 on v0

v1 whole, which is shorter than its diff:
```python
import functools

import jax
import jax.numpy as jnp
import numpy as np
from jax import lax
from jax.experimental import pallas as pl
from jax.experimental.pallas import tpu as pltpu
from jax.sharding import PartitionSpec as P

D = 8192
HEAD = 128
LAT = 2048
LEN = 1024
FEAT = 1024
EPSILON = 1e-05
ROPE_BASE = 500000.0
MESH = pl.DeviceIdType.MESH

RA = 48
RB = 128 - RA
N_IN = 128
N_OUT = 512 - N_IN
HALF = LAT // 2
N_COPIES = 104
BF = jnp.bfloat16
F32 = jnp.float32


def dot(a, b):
    return jnp.dot(a, b, preferred_element_type=F32)


def dot_t(a, b):
    return lax.dot_general(a, b, (((1,), (1,)), ((), ())), preferred_element_type=F32)


def rotated(u, cosine, sine):
    return u * cosine + pltpu.roll(u, HEAD // 2, 1) * sine


def kernel(
    acts_h, ana_h, syn_h, gain_h, wq_h, wkv_h, lg_h, cos_h, sin_h,
    att_h, grad_h,
    acts, ana, syn, gain, wq, wkv, cos, sin,
    part, lat, gl, sg, wp, wacc,
    ya, fb0, fb1, nb0, nb1, fa0, fa1, na0, na1, yb,
    ssv, ssall,
    lsem, ssem, rsem,
):
    p = lax.axis_index("pipe")
    dp = lax.axis_index("dp")
    t = lax.axis_index("tensor")
    z, yl = t // 2, t % 2
    yh, core = dp // 2, dp % 2
    oy = 1 - yl
    zf, zp, zm = (z + 2) % 4, (z + 1) % 4, (z + 3) % 4

    up = (p, dp, zp * 2 + yl)
    down = (p, dp, zm * 2 + yl)
    side = (p, dp, z * 2 + oy)
    outer = (p, (1 - yh) * 2 + core, z * 2 + oy)
    later = ((p + 1) % 4, dp, t)
    before = ((p + 3) % 4, dp, t)
    mate = (p, yh * 2 + 1 - core, t)
    across = (p, (1 - yh) * 2 + core, t)
    peers = [(p, dp, (t + i) % 8) for i in range(1, 8)]

    def rows_a(zz, y):
        return pl.ds(pl.multiple_of(zz * 256 + y * RA, 16), RA)

    def rows_b(zz, y):
        return pl.ds(pl.multiple_of(zz * 256 + 2 * RA + y * RB, 16), RB)

    def rows_bb(zz):
        return pl.ds(pl.multiple_of(zz * 256 + 2 * RA, 16), 2 * RB)

    def chunk(zz):
        return pl.ds(pl.multiple_of(zz * 256, 256), 256)

    lo, hi = pl.ds(0, HALF), pl.ds(HALF, HALF)

    key_cols, value_cols = pl.ds(512, HEAD), pl.ds(512 + HEAD, HEAD)

    def kv_at(zz):
        rows = pl.ds(pl.multiple_of(zz % 2 * 256, 256), 256)
        return rows, pl.ds(pl.multiple_of(zz // 2 * 256, 256), 128), pl.ds(pl.multiple_of(zz // 2 * 256 + 128, 128), 128)

    remote = []

    def send(src, dst, device):
        i = len(remote)
        copy = pltpu.make_async_remote_copy(
            src_ref=src, dst_ref=dst, send_sem=ssem.at[i], recv_sem=rsem.at[i],
            device_id=device, device_id_type=MESH,
        )
        copy.start()
        remote.append(copy)
        return copy

    n_local = [0]

    def local(src, dst):
        copy = pltpu.make_async_copy(src, dst, lsem.at[n_local[0]])
        n_local[0] += 1
        copy.start()
        return copy

    l_acts = local(acts_h, acts)
    l_ana = local(ana_h, ana)
    l_gain = local(gain_h, gain)
    l_syn = local(syn_h, syn)

    barrier = pltpu.get_barrier_semaphore()
    friends = peers + [outer, later, before, mate, across]
    for device in friends:
        pl.semaphore_signal(barrier, inc=1, device_id=device, device_id_type=MESH)
    pl.semaphore_wait(barrier, len(friends))

    g_shift_b = send(lg_h.at[pl.ds(RA, RB)], gl.at[rows_b(z, yl)], before)
    g_shift_a = send(lg_h.at[pl.ds(0, RA)], gl.at[rows_a(z, yl)], before)

    def encode(zz):
        @pl.loop(0, LAT // 512)
        def _(n):
            cols = pl.ds(pl.multiple_of(n * 512, 512), 512)
            part[chunk(zz), cols] = dot(acts[chunk(zz), :], ana[:, cols]).astype(BF)

    def fuse(k, first=False):
        rows = pl.ds(pl.multiple_of(k * FEAT, FEAT), FEAT)

        def add(cols, value):
            if first:
                wacc[:, cols] = value
            else:
                wacc[:, cols] += value

        @pl.loop(0, 2)
        def _(n):
            cols = pl.ds(pl.multiple_of(n * 256, 256), 256)
            add(cols, dot(sg[k], wq[rows, cols]))

        add(pl.ds(512, 256), dot(sg[k], wkv[rows, :]))

    eye = lax.broadcasted_iota(jnp.int32, (128, 128), 0) == lax.broadcasted_iota(jnp.int32, (128, 128), 1)

    def squares(zz):
        def step(n, total):
            cols = pl.ds(pl.multiple_of(n * 256, 256), 256)
            y = dot(lat[chunk(zz), :], syn[:, cols]).astype(BF).astype(F32)
            y = y * y
            return total + y[:, :128] + y[:, 128:]

        total = lax.fori_loop(0, FEAT // 256, step, jnp.zeros((256, 128), F32))
        column = jnp.sum(total, axis=1, keepdims=True)
        for i in range(2):
            ssv[zz * 2 + i] = jnp.sum(
                jnp.where(eye, column[i * 128:(i + 1) * 128], 0.0), axis=0, keepdims=True
            )

    def project(zz):
        rows = chunk(zz)

        @pl.loop(0, 2)
        def _(n):
            cols = pl.ds(pl.multiple_of(n * 256, 256), 256)
            y = dot(lat[rows, :], wp[:, cols])
            c, s = cos[rows, :], sin[rows, :]
            y = jnp.concatenate([rotated(y[:, :128], c, s), rotated(y[:, 128:], c, s)], axis=1)
            acts[rows, cols] = y.astype(BF)

        y = dot(lat[rows, :], wp[:, 512:768])
        kv_rows, k_cols, v_cols = kv_at(zz)
        wacc[kv_rows, k_cols] = rotated(y[:, :128], cos[rows, :], sin[rows, :])
        wacc[kv_rows, v_cols] = y[:, 128:]

    def scale_keys():
        @pl.loop(0, 4)
        def _(zz):
            kv_rows, k_cols, v_cols = kv_at(zz)
            for i in range(2):
                total = ssall[0, zz * 2 + i]
                for source in range(1, 8):
                    total = total + ssall[source, zz * 2 + i]
                scale = lax.rsqrt(total * (1.0 / D) + EPSILON)
                column = jnp.sum(jnp.where(eye, scale, 0.0), axis=1, keepdims=True)
                rows = pl.ds(pl.multiple_of(zz * 256 + i * 128, 128), 128)
                here = pl.ds(pl.multiple_of(zz % 2 * 256 + i * 128, 128), 128)
                acts[rows, key_cols] = (wacc[here, k_cols] * column).astype(BF)
                acts[rows, value_cols] = (wacc[here, v_cols] * column).astype(BF)
                s_cols = pl.ds(pl.multiple_of(512 + zz // 2 * 128, 128), 128)
                wacc[here, s_cols] = jnp.broadcast_to(column * HEAD ** (-0.5), (128, 128))

    def attend(h):
        cols = pl.ds(h * HEAD, HEAD)
        for i in range(4):
            end = 256 * (i + 1)
            rows = pl.ds(256 * i, 256)
            scores = dot_t(acts[rows, cols], acts[:end, key_cols])
            row = lax.broadcasted_iota(jnp.int32, (256, end), 0) + 256 * i
            col = lax.broadcasted_iota(jnp.int32, (256, end), 1)
            scores = jnp.where(col <= row, scores, -1e30)
            top = jnp.max(scores, axis=1, keepdims=True)
            factor = wacc[pl.ds(i % 2 * 256, 256), pl.ds(512 + i // 2 * 128, 1)]
            weights = jnp.exp((scores - top) * factor)
            total = jnp.sum(weights, axis=1, keepdims=True)
            mixed = dot(weights.astype(BF), acts[:end, value_cols])
            acts[rows, cols] = (mixed / total).astype(BF)

    outs = []

    def gradient(zz):
        @pl.loop(0, FEAT // 256)
        def _(n):
            cols = pl.ds(pl.multiple_of(n * 256, 256), 256)
            part[chunk(zz), cols] = dot_t(gl[chunk(zz), :], ana[cols, :]).astype(BF)

        for y in range(2):
            for src, off, size in ((rows_a(zz, y), 0, RA), (rows_b(zz, y), RA, RB)):
                dst = pl.ds(pl.multiple_of(zz * 256 + y * 128 + off, 16), size)
                outs.append(local(part.at[src, pl.ds(0, FEAT)], grad_h.at[dst, :]))

    def gather(x, own_a, own_b):
        own_b.wait_recv()
        b = rows_b(z, yl)
        b_side = send(x.at[b], x.at[b], side)
        b_up = send(x.at[b], x.at[b], up)
        b_down = send(x.at[b], x.at[b], down)
        own_a.wait_recv()
        a = rows_a(z, yl)
        a_up = send(x.at[a], x.at[a], up)
        a_down = send(x.at[a], x.at[a], down)
        a_side = [send(x.at[a], x.at[a], side)]
        yield
        b_side.wait_recv()
        b = rows_b(z, oy)
        c_up = send(x.at[b], x.at[b], up)
        c_down = send(x.at[b], x.at[b], down)
        yield
        a_up.wait_recv()
        a = rows_a(zm, yl)
        a_far0 = send(x.at[a, lo], x.at[a, lo], up)
        a_side.append(send(x.at[a], x.at[a], side))
        a_down.wait_recv()
        a = rows_a(zp, yl)
        a_far1 = send(x.at[a, hi], x.at[a, hi], down)
        a_side.append(send(x.at[a], x.at[a], side))
        yield
        b_up.wait_recv()
        c_up.wait_recv()
        b = rows_bb(zm)
        b_far0 = send(x.at[b, lo], x.at[b, lo], up)
        b_down.wait_recv()
        c_down.wait_recv()
        b = rows_bb(zp)
        b_far1 = send(x.at[b, hi], x.at[b, hi], down)
        yield
        a_far0.wait_recv()
        a_far1.wait_recv()
        a = rows_a(zf, yl)
        a_side.append(send(x.at[a], x.at[a], side))
        a_side[0].wait_recv()
        yield
        a_side[1].wait_recv()
        yield
        a_side[2].wait_recv()
        yield
        b_far0.wait_recv()
        b_far1.wait_recv()
        a_side[3].wait_recv()
        yield

    l_acts.wait()
    l_ana.wait()
    l_wq = local(wq_h, wq)
    l_wkv = local(wkv_h, wkv)
    l_cos = local(cos_h, cos)
    l_sin = local(sin_h, sin)
    encode(zf)
    bf_up = send(part.at[rows_bb(zf), lo], fb0, up)
    bf_down = send(part.at[rows_bb(zf), hi], fb1, down)
    y_a = [send(part.at[rows_a(zf, oy)], ya.at[0], side)]
    encode(zp)
    bn_up1 = send(part.at[rows_bb(zp), hi], nb0.at[:, hi], up)
    y_a.append(send(part.at[rows_a(zp, oy)], ya.at[1], side))
    encode(zm)
    bn_down0 = send(part.at[rows_bb(zm), lo], nb1.at[:, lo], down)
    y_a.append(send(part.at[rows_a(zm, oy)], ya.at[2], side))
    encode(z)
    y_a.append(send(part.at[rows_a(z, oy)], ya.at[3], side))

    l_gain.wait()
    l_syn.wait()
    in_start = pl.multiple_of(yh * (LAT - 2 * N_IN) + core * N_IN, 16)
    out_start = pl.multiple_of(jnp.where(yh == yl, 2 * N_IN, LAT // 2) + core * N_OUT, 16)
    scale = gain[:, pl.ds(pl.multiple_of(t * FEAT, FEAT), FEAT)]
    sg[t, :N_IN, :] = (syn[pl.ds(in_start, N_IN), :].astype(F32) * scale).astype(BF)
    sg[t, N_IN:, :] = (syn[pl.ds(out_start, N_OUT), :].astype(F32) * scale).astype(BF)

    near, far_half = pl.ds(0, N_IN), pl.ds(N_IN, N_OUT)

    def spread(k):
        return (
            send(sg.at[k, near], sg.at[k, near], side),
            send(sg.at[k, far_half], sg.at[k, far_half], outer),
        )

    s_up = send(sg.at[t], sg.at[t], up)
    s_down = send(sg.at[t], sg.at[t], down)
    s_own = spread(t)
    l_wq.wait()
    l_wkv.wait()
    fuse(t, first=True)

    bf_up.wait_recv()
    part[rows_bb(zp), lo] = part[rows_bb(zp), lo] + fb0[...]
    bn_up0 = send(part.at[rows_bb(zp), lo], nb0.at[:, lo], up)
    bf_down.wait_recv()
    part[rows_bb(zm), hi] = part[rows_bb(zm), hi] + fb1[...]
    bn_down1 = send(part.at[rows_bb(zm), hi], nb1.at[:, hi], down)

    def add_side(i, zz):
        y_a[i].wait_recv()
        part[rows_a(zz, yl), :] = part[rows_a(zz, yl), :] + ya[i]

    add_side(0, zf)
    af_up = send(part.at[rows_a(zf, yl), lo], fa0, up)
    af_down = send(part.at[rows_a(zf, yl), hi], fa1, down)
    add_side(1, zp)
    an_up1 = send(part.at[rows_a(zp, yl), hi], na0.at[:, hi], up)
    add_side(2, zm)
    an_down0 = send(part.at[rows_a(zm, yl), lo], na1.at[:, lo], down)
    add_side(3, z)

    for copy in (bn_up1, bn_down0, bn_up0, bn_down1):
        copy.wait_recv()

    def sum_b(y):
        here = pl.ds(pl.multiple_of(y * RB, 16), RB)
        return part[rows_b(z, y), :].astype(F32) + nb0[here, :].astype(F32) + nb1[here, :].astype(F32)

    part[rows_b(z, oy), :] = sum_b(oy).astype(BF)
    b_side = send(part.at[rows_b(z, oy)], yb, side)

    af_up.wait_recv()
    part[rows_a(zp, yl), lo] = part[rows_a(zp, yl), lo] + fa0[...]
    an_up0 = send(part.at[rows_a(zp, yl), lo], na0.at[:, lo], up)
    af_down.wait_recv()
    part[rows_a(zm, yl), hi] = part[rows_a(zm, yl), hi] + fa1[...]
    an_down1 = send(part.at[rows_a(zm, yl), hi], na1.at[:, hi], down)

    quarter0, quarter1 = pl.ds(0, FEAT // 2), pl.ds(FEAT // 2, FEAT // 2)
    s_up.wait_recv()
    k = zm * 2 + yl
    sf_up = send(sg.at[k, :, quarter0], sg.at[k, :, quarter0], up)
    s_m = spread(k)
    s_down.wait_recv()
    k = zp * 2 + yl
    sf_down = send(sg.at[k, :, quarter1], sg.at[k, :, quarter1], down)
    s_p = spread(k)

    b_side.wait_recv()
    part[rows_b(z, yl), :] = (sum_b(yl) + yb[...].astype(F32)).astype(BF)
    r_shift_b = send(part.at[rows_b(z, yl)], lat.at[rows_b(z, yl)], later)
    for copy in (an_up1, an_down0, an_up0, an_down1):
        copy.wait_recv()
    part[rows_a(z, yl), :] = (
        part[rows_a(z, yl), :].astype(F32) + na0[...].astype(F32) + na1[...].astype(F32)
    ).astype(BF)
    r_shift_a = send(part.at[rows_a(z, yl)], lat.at[rows_a(z, yl)], later)

    fuse(zm * 2 + yl)
    fuse(zp * 2 + yl)
    sf_up.wait_recv()
    sf_down.wait_recv()
    s_f = spread(zf * 2 + yl)

    gather_l = gather(lat, r_shift_a, r_shift_b)
    gather_g = gather(gl, g_shift_a, g_shift_b)
    next(gather_l)
    next(gather_g)
    fuse(zf * 2 + yl)
    for copies, zz in ((s_own, z), (s_m, zm), (s_p, zp)):
        for copy in copies:
            copy.wait_recv()
        fuse(zz * 2 + oy)
    next(gather_l)
    next(gather_g)
    for copy in s_f:
        copy.wait_recv()
    fuse(zf * 2 + oy)

    mine = (pl.ds(in_start, N_IN), pl.ds(out_start, N_OUT))
    wp[mine[0], :] = wacc[:N_IN, :].astype(BF)
    wp[mine[1], :] = wacc[N_IN:, :].astype(BF)
    w_mate = [send(wp.at[rows], wp.at[rows], mate) for rows in mine]
    w_across = [send(wp.at[rows], wp.at[rows], across) for rows in mine]
    next(gather_l)
    next(gather_l)
    next(gather_g)
    next(gather_g)
    for copy in w_across:
        copy.wait_recv()
    a_in = pl.multiple_of((1 - yh) * (LAT - 2 * N_IN) + core * N_IN, 16)
    a_out = pl.multiple_of(jnp.where(yh != yl, 2 * N_IN, LAT // 2) + core * N_OUT, 16)
    theirs = (pl.ds(a_in, N_IN), pl.ds(a_out, N_OUT))
    w_relay = [send(wp.at[rows], wp.at[rows], mate) for rows in theirs]
    next(gather_l)
    squares(z)
    next(gather_l)
    squares(zm)
    next(gather_l)
    squares(zp)
    for copy in w_mate + w_relay:
        copy.wait_recv()
    l_cos.wait()
    l_sin.wait()
    project(z)
    project(zm)
    project(zp)
    next(gather_g)
    next(gather_l)
    squares(zf)
    ssall[t] = ssv[...]
    ss_copies = [send(ssv, ssall.at[t], device) for device in peers]
    project(zf)
    for copy in ss_copies:
        copy.wait_recv()
    scale_keys()

    for h in range(4):
        attend(h)
    l_att = local(acts.at[:, pl.ds(0, 512)], att_h)
    for copy in remote:
        copy.wait_send()
    gradient(z)
    next(gather_g)
    gradient(zm)
    next(gather_g)
    gradient(zp)
    next(gather_g)
    gradient(zf)
    l_att.wait()
    for copy in outs:
        copy.wait()


def tables():
    frequency = ROPE_BASE ** (-(np.arange(HEAD // 2) * 2.0 / HEAD))
    angles = np.arange(LEN)[:, None] * frequency[None, :]
    cosine, sine = np.cos(angles), np.sin(angles)
    return (
        np.concatenate([cosine, cosine], axis=1).astype(np.float32),
        np.concatenate([-sine, sine], axis=1).astype(np.float32),
    )


def on_device(activations, analysis, synthesis, norm_gain, query_weight, keys_values, latent_grad):
    cos, sin = tables()
    anywhere = pl.BlockSpec(memory_space=pl.ANY)

    def vmem(*shape, dtype=BF):
        return pltpu.VMEM(shape, dtype)

    attended, grad = pl.pallas_call(
        kernel,
        out_shape=(
            jax.ShapeDtypeStruct((LEN, 512), BF),
            jax.ShapeDtypeStruct((LEN, FEAT), BF),
        ),
        in_specs=[anywhere] * 9,
        out_specs=(anywhere, anywhere),
        scratch_shapes=[
            vmem(LEN, FEAT), vmem(FEAT, LAT), vmem(LAT, FEAT), vmem(1, D, dtype=F32),
            vmem(D, 512), vmem(D, 256), vmem(LEN, HEAD, dtype=F32), vmem(LEN, HEAD, dtype=F32),
            vmem(LEN, LAT), vmem(LEN, LAT), vmem(LEN, LAT), vmem(8, 512, FEAT), vmem(LAT, 768),
            vmem(512, 768, dtype=F32),
            vmem(4, RA, LAT), vmem(2 * RB, HALF), vmem(2 * RB, HALF), vmem(2 * RB, LAT), vmem(2 * RB, LAT),
            vmem(RA, HALF), vmem(RA, HALF), vmem(RA, LAT), vmem(RA, LAT),
            vmem(RB, LAT),
            vmem(8, 1, 128, dtype=F32), vmem(8, 8, 1, 128, dtype=F32),
            pltpu.SemaphoreType.DMA((32,)),
            pltpu.SemaphoreType.DMA((N_COPIES,)),
            pltpu.SemaphoreType.DMA((N_COPIES,)),
        ],
        compiler_params=pltpu.CompilerParams(
            collective_id=0, has_side_effects=True, vmem_limit_bytes=63 * 2**20
        ),
        cost_estimate=pl.CostEstimate(flops=28 * 10**9, bytes_accessed=30 * 10**6, transcendentals=0),
    )(
        activations[0, 0], analysis[0], synthesis[0], norm_gain, query_weight[0], keys_values[0],
        latent_grad[0, 0], jnp.asarray(cos), jnp.asarray(sin),
    )
    return attended[None, None], grad[None, None]


def solution(mesh):
    return jax.shard_map(
        on_device,
        mesh=mesh,
        in_specs=(
            P("pipe", "dp", None, "tensor"),
            P("pipe", "tensor", None),
            P("pipe", None, "tensor"),
            P("pipe", None),
            P("pipe", None, "tensor"),
            P("pipe", None, "tensor"),
            P("pipe", "dp", "tensor", None),
        ),
        out_specs=(P("pipe", "dp", None, "tensor"), P("pipe", "dp", None, "tensor")),
        check_vma=False,
    )
```

time: 765 us -> 181 us (0.24)
  waiting for transfers between devices: 638 us -> 0 us
  Pallas kernels: 0 us -> 175 us
  matrix products: 57.5 us -> 0 us
  local copies, waits for them, and re-layouts: 24.4 us -> 5.34 us
  blocking collectives: 17.9 us -> 0 us
  between operations: 14 us -> 0.64 us
  other arithmetic: 9.92 us -> 0 us
    all_gather x3 -> x0, waiting for transfers between devices: 440 us -> none  [the longest x1 318 us: on_device(): portion = lax.all_gather(normed, 'tensor', axis=1, tiled=True)]
    pallas_call x0 -> x1, Pallas kernels: none -> 175 us  [on_device(): pl.pallas_call(kernel, out_shape=(jax.ShapeDtypeStruct((LEN, 512), BF), j...]
    reduce_scatter x1 -> x0, waiting for transfers between devices: 172 us -> none  [on_device(): lax.psum_scatter(jnp.dot(acts_local, w_analysis, preferred_element_type=j...]
    dot_general x9 -> x0, matrix products: 57.5 us -> none  [the longest x1 14.5 us: on_device(): queries_all = jnp.dot(portion, w_query, preferred_element_type=jnp.float32)]
    ppermute x2 -> x0, waiting for transfers between devices: 26.3 us -> none  [passed_along(): return lax.ppermute(value, axis, pairs)]
    psum x1 -> x0, blocking collectives: 17.9 us -> none  [on_device(): squares = lax.psum(jnp.sum(synth_float * synth_float, axis=1), 'tensor')]
    dot_general x1 -> x0, local copies, waits for them, and re-layouts: 11.9 us -> none  [on_device(): queries_all = jnp.dot(portion, w_query, preferred_element_type=jnp.float32)]
  transfers between devices with their start and end apart: 6 -> 0, of which waited for: 6 -> 0; matrix products, arithmetic and copies ran while one was open for 5% -> 0% of each run, Pallas kernels for 0% -> 0%
where the time goes in v1:
time: 181 us
  Pallas kernels  175 us (97%)
  local copies, waits for them, and re-layouts  5.34 us (3%)
    pallas_call x1, Pallas kernels, on_device(): pl.pallas_call(kernel, out_shape=(jax.ShapeDtypeStruct((LEN, 512), BF), j...  175 us
    unnamed x2, local copies, waits for them, and re-layouts  5.34 us

profile of v1, /device:TPU:6, one launch (start us, length us, event | category | flops | bytes accessed | tf_op | source)
XLA Modules:
  0.0 180.5 jit_solution(4814414255070795765)
XLA Ops:
  0.6 174.5 %shard_map.104 = (bf16[1024,512]{1,0:T(8,128)(2,1)}, bf16[1024,1024]{1,0:T(8,128)(2,1)}) custom-call(bf16[1024,1024]{1,0:T(8,128)(2,1)} %bitcast.14, bf16[1024,2048]{1,0:T(8,128)(2,1)} %bitcast.11, bf16[2048,1024]{1,0:T(8,128)(2,1)} %bitcast.12, f32[1,8192]{1,0:T(1,128)} %gain_h.1, bf16[8192,512]{1,0:T(8,128)(2,1)} %bitcast.10, bf16[8192,256]{1,0:T(8,128)(2,1)} %bitcast.13, ...), custom_call_target="tpu_custom_call" | custom-call | flops 28000000000 | bytes 30000000 | tf_op jit(solution)/shard_map/pallas_call | solution.py:465
  175.2 2.3 %copy.13 = bf16[1,1,1024,512]{3,2,1,0:T(8,128)(2,1)} copy(bf16[1,1,1024,512]{3,2,1,0:T(8,128)(2,1)} %bitcast.9) | data formatting | bytes 2097152
  177.4 3.1 %copy.14 = bf16[1,1,1024,1024]{3,2,1,0:T(8,128)(2,1)} copy(bf16[1,1,1024,1024]{3,2,1,0:T(8,128)(2,1)} %bitcast.8) | data formatting | bytes 4194304

commit v2 on v0

v2 whole, which is shorter than its diff:
```python
import functools

import jax
import jax.numpy as jnp
import numpy as np
from jax import lax
from jax.experimental import pallas as pl
from jax.experimental.pallas import tpu as pltpu
from jax.sharding import PartitionSpec as P

D = 8192
HEAD = 128
LAT = 2048
LEN = 1024
FEAT = 1024
EPSILON = 1e-05
LOG2_E = 1.4426950408889634
ROPE_BASE = 500000.0
MESH = pl.DeviceIdType.MESH

RA = 48
RB = 128 - RA
RG = 48
N_IN = 128
N_OUT = 512 - N_IN


def pieces_of():
    out = []
    for q in range(4):
        cut = min(max(N_IN, q * 128), q * 128 + 128)
        parts = [("in", q * 128, cut - q * 128), ("out", cut, q * 128 + 128 - cut)]
        out.append(tuple(part for part in parts if part[2]))
    return tuple(out)


PIECES = pieces_of()
HALF = LAT // 2
N_COPIES = 144
BF = jnp.bfloat16
F32 = jnp.float32


def dot(a, b):
    return jnp.dot(a, b, preferred_element_type=F32)


def dot_t(a, b):
    return lax.dot_general(a, b, (((1,), (1,)), ((), ())), preferred_element_type=F32)


def rotated(u, cosine, sine):
    return u * cosine + pltpu.roll(u, HEAD // 2, 1) * sine


ORDER = [
    16, 31, 15, 41, 17, 0, 56, 1, 24, 2, 27, 36, 22, 20, 5, 4, 3, 35, 6, 19, 7, 9, 8, 21, 45, 29, 12, 28, 18, 10,
    11, 47, 49, 34, 26, 25, 50, 38, 23, 14, 13, 30, 75, 32, 33, 42, 48, 60, 68, 40, 39, 67, 43, 37, 57, 51, 70, 59,
    71, 46, 69, 44, 61, 62, 58, 52, 53, 63, 64, 74, 83, 76, 72, 73, 86, 77, 54, 89, 65, 55, 66, 92, 95, 79, 90, 84,
    78, 87, 93, 80, 81, 85, 96, 99, 103, 104, 82, 102, 98, 101, 97, 100, 88, 105, 91, 94,
]


class Names:
    def __getattr__(self, name):
        return name


K = Names()


def join(*parts):
    return "".join(str(part) for part in parts)


def kernel(
    acts_h, ana_h, syn_h, gain_h, wq_h, wkv_h, lg_h, cos_h, sin_h,
    att_h, grad_h,
    acts, ana, syn, gain, wq, wkv, cos, sin,
    part, lat, gl, sg, wp, wacc,
    ya, fb0, fb1, nb0, nb1, fa0, fa1, na0, na1, yb,
    ssv, ssall,
    lsem, ssem, rsem,
):
    p = lax.axis_index("pipe")
    dp = lax.axis_index("dp")
    t = lax.axis_index("tensor")
    z, yl = t // 2, t % 2
    yh, core = dp // 2, dp % 2
    oy = 1 - yl
    at_z = {"o": z, "p": (z + 1) % 4, "m": (z + 3) % 4, "f": (z + 2) % 4}

    up = (p, dp, at_z["p"] * 2 + yl)
    down = (p, dp, at_z["m"] * 2 + yl)
    side = (p, dp, z * 2 + oy)
    outer = (p, (1 - yh) * 2 + core, z * 2 + oy)
    later = ((p + 1) % 4, dp, t)
    before = ((p + 3) % 4, dp, t)
    mate = (p, yh * 2 + 1 - core, t)
    across = (p, (1 - yh) * 2 + core, t)
    peers = [(p, dp, (t + i) % 8) for i in range(1, 8)]

    def rows_a(zz, y, ra=RA):
        return pl.ds(pl.multiple_of(zz * 256 + y * ra, 16), ra)

    def rows_b(zz, y, ra=RA):
        return pl.ds(pl.multiple_of(zz * 256 + 2 * ra + y * (128 - ra), 16), 128 - ra)

    def rows_bb(zz, ra=RA):
        return pl.ds(pl.multiple_of(zz * 256 + 2 * ra, 16), 256 - 2 * ra)

    def chunk(zz):
        return pl.ds(pl.multiple_of(zz * 256, 256), 256)

    lo, hi = pl.ds(0, HALF), pl.ds(HALF, HALF)

    key_cols, value_cols = pl.ds(512, HEAD), pl.ds(512 + HEAD, HEAD)

    def kv_at(zz):
        rows = pl.ds(pl.multiple_of(zz % 2 * 256, 256), 256)
        cols = zz // 2 * 256
        return rows, pl.ds(pl.multiple_of(cols, 256), 128), pl.ds(pl.multiple_of(cols + 128, 128), 128)

    remote = {}
    arrived = set()

    def send(name, src, dst, device):
        i = len(remote)
        copy = pltpu.make_async_remote_copy(
            src_ref=src, dst_ref=dst, send_sem=ssem.at[i], recv_sem=rsem.at[i],
            device_id=device, device_id_type=MESH,
        )
        copy.start()
        remote[name] = copy

    def arrive(name):
        if name not in arrived:
            arrived.add(name)
            remote[name].wait_recv()

    local_copies = {}

    def local(name, src, dst):
        copy = pltpu.make_async_copy(src, dst, lsem.at[len(local_copies)])
        copy.start()
        local_copies[name] = copy

    def loaded(name):
        if name not in arrived:
            arrived.add(name)
            local_copies[name].wait()

    def encode(zz):
        @pl.loop(0, LAT // 512, unroll=True)
        def _(n):
            cols = pl.ds(pl.multiple_of(n * 512, 512), 512)
            part[chunk(zz), cols] = dot(acts[chunk(zz), :], ana[:, cols]).astype(BF)

    started = []

    def fuse(k, j):
        rows = pl.ds(pl.multiple_of(k * FEAT, FEAT), FEAT)
        here = pl.ds(j * 256, 256)

        def add(cols, value):
            if j not in started:
                wacc[here, cols] = value
            else:
                wacc[here, cols] += value

        @pl.loop(0, 2, unroll=True)
        def _(n):
            cols = pl.ds(pl.multiple_of(n * 256, 256), 256)
            add(cols, dot(sg[k, here, :], wq[rows, cols]))

        add(pl.ds(512, 256), dot(sg[k, here, :], wkv[rows, :]))

    def diagonal():
        return lax.broadcasted_iota(jnp.int32, (128, 128), 0) == lax.broadcasted_iota(jnp.int32, (128, 128), 1)

    def squares(zz):
        def step(n, total):
            cols = pl.ds(pl.multiple_of(n * 256, 256), 256)
            y = dot(lat[chunk(zz), :], syn[:, cols]).astype(BF).astype(F32)
            y = y * y
            return total + y[:, :128] + y[:, 128:]

        total = lax.fori_loop(0, FEAT // 256, step, jnp.zeros((256, 128), F32), unroll=True)
        column = jnp.sum(total, axis=1, keepdims=True)
        for i in range(2):
            ssv[zz * 2 + i] = jnp.sum(
                jnp.where(diagonal(), column[i * 128:(i + 1) * 128], 0.0), axis=0, keepdims=True
            )

    def project(zz):
        rows = chunk(zz)

        @pl.loop(0, 2, unroll=True)
        def _(n):
            cols = pl.ds(pl.multiple_of(n * 256, 256), 256)
            y = dot(lat[rows, :], wp[:, cols])
            c, s = cos[rows, :], sin[rows, :]
            y = jnp.concatenate([rotated(y[:, :128], c, s), rotated(y[:, 128:], c, s)], axis=1)
            acts[rows, cols] = y.astype(BF)

        y = dot(lat[rows, :], wp[:, 512:768])
        kv_rows, k_cols, v_cols = kv_at(zz)
        wacc[kv_rows, k_cols] = rotated(y[:, :128], cos[rows, :], sin[rows, :])
        wacc[kv_rows, v_cols] = y[:, 128:]

    def scale_keys():
        @pl.loop(0, 4)
        def _(zz):
            kv_rows, k_cols, v_cols = kv_at(zz)
            for i in range(2):
                total = ssall[0, zz * 2 + i]
                for source in range(1, 8):
                    total = total + ssall[source, zz * 2 + i]
                scale = lax.rsqrt(total * (1.0 / D) + EPSILON)
                column = jnp.sum(jnp.where(diagonal(), scale, 0.0), axis=1, keepdims=True)
                rows = pl.ds(pl.multiple_of(zz * 256 + i * 128, 128), 128)
                here = pl.ds(pl.multiple_of(zz % 2 * 256 + i * 128, 128), 128)
                acts[rows, key_cols] = (wacc[here, k_cols] * column).astype(BF)
                acts[rows, value_cols] = (wacc[here, v_cols] * column).astype(BF)
                s_cols = pl.ds(pl.multiple_of(512 + zz // 2 * 128, 128), 128)
                wacc[here, s_cols] = jnp.broadcast_to(column * (HEAD ** (-0.5) * LOG2_E), (128, 128))

    def attend(h, blocks):
        cols = pl.ds(h * HEAD, HEAD)
        for i in blocks:
            end = 256 * (i + 1)
            rows = pl.ds(256 * i, 256)
            scores = dot_t(acts[rows, cols], acts[:end, key_cols])
            row = lax.broadcasted_iota(jnp.int32, (256, end), 0) + 256 * i
            col = lax.broadcasted_iota(jnp.int32, (256, end), 1)
            scores = jnp.where(col <= row, scores, -1e30)
            top = jnp.max(scores, axis=1, keepdims=True)
            factor = wacc[pl.ds(i % 2 * 256, 256), pl.ds(512 + i // 2 * 128, 1)]
            weights = jnp.exp2((scores - top) * factor)
            total = jnp.sum(weights, axis=1, keepdims=True)
            mixed = dot(weights.astype(BF), acts[:end, value_cols])
            acts[rows, cols] = (mixed / total).astype(BF)

    def gradient(zz):
        @pl.loop(0, FEAT // 256, unroll=True)
        def _(n):
            cols = pl.ds(pl.multiple_of(n * 256, 256), 256)
            part[chunk(zz), cols] = dot_t(gl[chunk(zz), :], ana[cols, :]).astype(BF)

    steps = {}

    def step(name, copies=(), after=(), kind=""):
        def register(body):
            steps[name] = (tuple(copies), tuple(after), kind, body)
            return body

        return register

    @step(K.enc_f)
    def _():
        loaded(K.acts)
        loaded(K.ana)
        local(K.wq, wq_h, wq)
        local(K.wkv, wkv_h, wkv)
        local(K.cos, cos_h, cos)
        local(K.sin, sin_h, sin)
        encode(at_z["f"])
        send(K.bf_up, part.at[rows_bb(at_z["f"]), lo], fb0, up)
        send(K.bf_dn, part.at[rows_bb(at_z["f"]), hi], fb1, down)
        send(K.ya_f, part.at[rows_a(at_z["f"], oy)], ya.at[0], side)

    @step(K.enc_p, after=[K.enc_f])
    def _():
        encode(at_z["p"])
        send(K.bn_up1, part.at[rows_bb(at_z["p"]), hi], nb0.at[:, hi], up)
        send(K.ya_p, part.at[rows_a(at_z["p"], oy)], ya.at[1], side)

    @step(K.enc_m, after=[K.enc_p])
    def _():
        encode(at_z["m"])
        send(K.bn_dn0, part.at[rows_bb(at_z["m"]), lo], nb1.at[:, lo], down)
        send(K.ya_m, part.at[rows_a(at_z["m"], oy)], ya.at[2], side)

    @step(K.enc_o, after=[K.enc_m])
    def _():
        encode(at_z["o"])
        send(K.ya_o, part.at[rows_a(at_z["o"], oy)], ya.at[3], side)

    @step(K.rb_up, [K.bf_up], [K.enc_p])
    def _():
        here = (rows_bb(at_z["p"]), lo)
        part[here] = part[here] + fb0[...]
        send(K.bn_up0, part.at[here], nb0.at[:, lo], up)

    @step(K.rb_dn, [K.bf_dn], [K.enc_m])
    def _():
        here = (rows_bb(at_z["m"]), hi)
        part[here] = part[here] + fb1[...]
        send(K.bn_dn1, part.at[here], nb1.at[:, hi], down)

    def add_side(i, w):
        here = rows_a(at_z[w], yl)
        part[here, :] = part[here, :] + ya[i]

    @step(K.ra_f, [K.ya_f], [K.enc_f])
    def _():
        add_side(0, "f")
        send(K.af_up, part.at[rows_a(at_z["f"], yl), lo], fa0, up)
        send(K.af_dn, part.at[rows_a(at_z["f"], yl), hi], fa1, down)

    @step(K.ra_p, [K.ya_p], [K.enc_p])
    def _():
        add_side(1, "p")
        send(K.an_up1, part.at[rows_a(at_z["p"], yl), hi], na0.at[:, hi], up)

    @step(K.ra_m, [K.ya_m], [K.enc_m])
    def _():
        add_side(2, "m")
        send(K.an_dn0, part.at[rows_a(at_z["m"], yl), lo], na1.at[:, lo], down)

    @step(K.ra_o, [K.ya_o], [K.enc_o])
    def _():
        add_side(3, "o")

    @step(K.ra_up, [K.af_up], [K.ra_p])
    def _():
        here = (rows_a(at_z["p"], yl), lo)
        part[here] = part[here] + fa0[...]
        send(K.an_up0, part.at[here], na0.at[:, lo], up)

    @step(K.ra_dn, [K.af_dn], [K.ra_m])
    def _():
        here = (rows_a(at_z["m"], yl), hi)
        part[here] = part[here] + fa1[...]
        send(K.an_dn1, part.at[here], na1.at[:, hi], down)

    def sum_b(y):
        here = pl.ds(pl.multiple_of(y * RB, 16), RB)
        return part[rows_b(z, y), :].astype(F32) + nb0[here, :].astype(F32) + nb1[here, :].astype(F32)

    @step(K.b_sum, [K.bn_up0, K.bn_up1, K.bn_dn0, K.bn_dn1], [K.enc_o])
    def _():
        part[rows_b(z, oy), :] = sum_b(oy).astype(BF)
        send(K.yb, part.at[rows_b(z, oy)], yb, side)

    @step(K.b_red, [K.yb], [K.b_sum])
    def _():
        part[rows_b(z, yl), :] = (sum_b(yl) + yb[...].astype(F32)).astype(BF)
        send(K.l_shift_b, part.at[rows_b(z, yl)], lat.at[rows_b(z, yl)], later)

    @step(K.a_red, [K.an_up0, K.an_up1, K.an_dn0, K.an_dn1], [K.ra_o])
    def _():
        part[rows_a(z, yl), :] = (
            part[rows_a(z, yl), :].astype(F32) + na0[...].astype(F32) + na1[...].astype(F32)
        ).astype(BF)
        send(K.l_shift_a, part.at[rows_a(z, yl)], lat.at[rows_a(z, yl)], later)

    def place(segment, group):
        kind, first, size = segment
        if kind == "in":
            at = group * (LAT - 2 * N_IN) + core * N_IN + first
        else:
            at = (N_IN * 2 + (group + yl) % 2 * (LAT // 2 - 2 * N_IN)) + core * N_OUT + first - N_IN
        return pl.multiple_of(at, 16)

    def scale_step(j):
        @step(join(K.s_scale, j), kind="s")
        def _():
            loaded(K.gain)
            loaded(K.syn)
            scale = gain[:, pl.ds(pl.multiple_of(t * FEAT, FEAT), FEAT)]
            for q in (2 * j, 2 * j + 1):
                for segment in PIECES[q]:
                    _, first, size = segment
                    rows = pl.ds(place(segment, yh), size)
                    sg[t, pl.ds(first, size), :] = (syn[rows, :].astype(F32) * scale).astype(BF)

    def column(w):
        return at_z[w] * 2 + yl

    quarters = pl.ds(0, FEAT // 2), pl.ds(FEAT // 2, FEAT // 2)

    sources = {"o": [], "m": [K.s_up], "p": [K.s_dn], "f": [K.s_far_up, K.s_far_dn]}
    earlier = {"o": [K.s_scale], "m": [K.s_z], "p": [K.s_z], "f": [K.s_fu, K.s_fd]}

    def fill(names, q):
        return [join(name, q // 2 if name == K.s_scale else q) for name in names]

    def synthesis_steps(q):
        rows = pl.ds(q * 128, 128)

        @step(join(K.s_z, q), after=[join(K.s_scale, q // 2)], kind="s")
        def _():
            send(join(K.s_up, q), sg.at[t, rows], sg.at[t, rows], up)
            send(join(K.s_dn, q), sg.at[t, rows], sg.at[t, rows], down)

        @step(join(K.s_fu, q), [join(K.s_up, q)], [join(K.s_z, q)], kind="s")
        def _():
            k = column("m")
            send(join(K.s_far_up, q), sg.at[k, rows, quarters[0]], sg.at[k, rows, quarters[0]], up)

        @step(join(K.s_fd, q), [join(K.s_dn, q)], [join(K.s_z, q)], kind="s")
        def _():
            k = column("p")
            send(join(K.s_far_dn, q), sg.at[k, rows, quarters[1]], sg.at[k, rows, quarters[1]], down)

        for w in "ompf":
            for kind, first, size in PIECES[q]:
                def spread(w=w, kind=kind, first=first, size=size):
                    ref = sg.at[column(w), pl.ds(first, size)]
                    send(join(K.s_, kind, "_", w, q), ref, ref, side if kind == "in" else outer)

                step(join(K.s_y, kind, "_", w, q), fill(sources[w], q), fill(earlier[w], q), kind="s")(spread)

    def fuse_steps(j):
        both = (2 * j, 2 * j + 1)

        def fuse_into(k):
            loaded(K.wq)
            loaded(K.wkv)
            fuse(k, j)
            started.append(j)

        for w in "ompf":
            def own(w=w):
                fuse_into(column(w))

            def others(w=w):
                fuse_into(at_z[w] * 2 + oy)

            copies = [name for q in both for name in fill(sources[w], q)]
            after = [name for q in both for name in fill(earlier[w], q)]
            step(join(K.u_, w, j), copies, [K.enc_f] + after, kind=K.fuse)(own)
            parts = [join(part[0], "_", w, q) for q in both for part in PIECES[q]]
            step(
                join(K.t_, w, j), [K.s_ + part for part in parts], [K.enc_f] + [K.s_y + part for part in parts], kind=K.fuse
            )(others)

        @step(join(K.w_out, j), after=[join(u, w, j) for u in (K.u_, K.t_) for w in "ompf"])
        def _():
            for q in both:
                for segment in PIECES[q]:
                    kind, first, size = segment
                    mine = pl.ds(place(segment, yh), size)
                    wp[mine, :] = wacc[first:first + size, :].astype(BF)
                    send(join(K.w_across, kind, q), wp.at[mine], wp.at[mine], across)
                    send(join(K.w_mate, kind, q), wp.at[mine], wp.at[mine], mate)

        for q in both:
            for segment in PIECES[q]:
                def relay(q=q, segment=segment):
                    theirs = pl.ds(place(segment, 1 - yh), segment[2])
                    send(join(K.w_last, segment[0], q), wp.at[theirs], wp.at[theirs], mate)

                step(join(K.w_relay, segment[0], q), [join(K.w_across, segment[0], q)], [join(K.w_out, j)])(relay)

    for j in range(2):
        scale_step(j)
    for q in range(4):
        synthesis_steps(q)
    for j in range(2):
        fuse_steps(j)

    fused = [join(part[0], q) for q in range(4) for part in PIECES[q]]

    def gather_steps(g, x, first, ra):
        def pass_on(name, where, device, cols=None):
            ref = x.at[where] if cols is None else x.at[where, cols]
            send(g + name, ref, ref, device)

        @step(g + K.b0, [g + K.shift_b], first, kind=g)
        def _():
            here = rows_b(z, yl, ra)
            pass_on(K.b_side, here, side)
            pass_on(K.b_up, here, up)
            pass_on(K.b_dn, here, down)

        @step(g + K.a0, [g + K.shift_a], first, kind=g)
        def _():
            here = rows_a(z, yl, ra)
            pass_on(K.a_up, here, up)
            pass_on(K.a_dn, here, down)
            pass_on(K.a_side_o, here, side)

        @step(g + K.b1, [g + K.b_side], [g + K.b0], kind=g)
        def _():
            here = rows_b(z, oy, ra)
            pass_on(K.c_up, here, up)
            pass_on(K.c_dn, here, down)

        @step(g + K.am, [g + K.a_up], [g + K.a0], kind=g)
        def _():
            here = rows_a(at_z["m"], yl, ra)
            pass_on(K.a_far_up, here, up, lo)
            pass_on(K.a_side_m, here, side)

        @step(g + K.ap, [g + K.a_dn], [g + K.a0], kind=g)
        def _():
            here = rows_a(at_z["p"], yl, ra)
            pass_on(K.a_far_dn, here, down, hi)
            pass_on(K.a_side_p, here, side)

        @step(g + K.bm, [g + K.b_up, g + K.c_up], [g + K.b1], kind=g)
        def _():
            pass_on(K.b_far_up, rows_bb(at_z["m"], ra), up, lo)

        @step(g + K.bp, [g + K.b_dn, g + K.c_dn], [g + K.b1], kind=g)
        def _():
            pass_on(K.b_far_dn, rows_bb(at_z["p"], ra), down, hi)

        @step(g + K.af, [g + K.a_far_up, g + K.a_far_dn], [g + K.am, g + K.ap], kind=g)
        def _():
            pass_on(K.a_side_f, rows_a(at_z["f"], yl, ra), side)

    gather_steps(K.l_, lat, [K.a_red, K.b_red], RA)
    gather_steps(K.g_, gl, [], RG)

    def whole(g, w):
        copies, after = {
            "o": ([K.shift_a, K.shift_b, K.b_side, K.a_side_o], [K.b0, K.a0]),
            "m": ([K.b_up, K.c_up, K.a_up, K.a_side_m], [K.b1, K.am]),
            "p": ([K.b_dn, K.c_dn, K.a_dn, K.a_side_p], [K.b1, K.ap]),
            "f": ([K.b_far_up, K.b_far_dn, K.a_far_up, K.a_far_dn, K.a_side_f], [K.bm, K.bp, K.af]),
        }[w]
        return [g + name for name in copies], [g + name for name in after]

    def token_steps(w):
        copies, after = whole(K.l_, w)

        @step(K.sq_ + w, copies, after, kind=K.squares)
        def _():
            squares(at_z[w])

        @step(K.pr_ + w, copies + [c + i for c in (K.w_mate, K.w_last) for i in fused],
              after + [K.w_relay + i for i in fused], kind=K.project)
        def _():
            loaded(K.cos)
            loaded(K.sin)
            project(at_z[w])

        copies, after = whole(K.g_, w)

        @step(K.gr_ + w, copies, after + [K.pr_ + u for u in "ompf"], kind=K.gradient)
        def _():
            if not flushed:
                flushed.append(w)
                for name in part_sends:
                    remote[name].wait_send()
            zz = at_z[w]
            gradient(zz)
            for y in range(2):
                for part_name, src, off, size in (("a", rows_a(zz, y, RG), 0, RG), ("b", rows_b(zz, y, RG), RG, 128 - RG)):
                    dst = pl.ds(pl.multiple_of(zz * 256 + y * 128 + off, 16), size)
                    local(join(K.out_, w, y, part_name), part.at[src, pl.ds(0, FEAT)], grad_h.at[dst, :])

    flushed = []
    part_sends = [
        K.bf_up, K.bf_dn, K.ya_f, K.bn_up1, K.ya_p, K.bn_dn0, K.ya_m, K.ya_o, K.bn_up0, K.bn_dn1, K.af_up, K.af_dn,
        K.an_up1, K.an_dn0, K.an_up0, K.an_dn1, K.yb, K.l_shift_b, K.l_shift_a,
    ]
    for w in "ompf":
        token_steps(w)

    ss_names = [join(K.ss, i) for i in range(7)]

    @step(K.ss, after=[K.sq_ + w for w in "ompf"])
    def _():
        ssall[t] = ssv[...]
        for name, device in zip(ss_names, peers):
            send(name, ssv, ssall.at[t], device)

    @step(K.keys, ss_names, [K.ss] + [K.pr_ + w for w in "ompf"], kind=K.keys)
    def _():
        scale_keys()

    def attend_step(h, j):
        @step(join(K.at_, h, j), after=[K.keys], kind=K.attend)
        def _():
            attend(h, ((0, 3), (1, 2))[j])

    for h in range(4):
        for j in range(2):
            attend_step(h, j)

    @step(K.att, after=[join(K.at_, h, j) for h in range(4) for j in range(2)], kind=K.attend)
    def _():
        local(K.att, acts.at[:, pl.ds(0, 512)], att_h)

    local(K.acts, acts_h, acts)
    local(K.ana, ana_h, ana)
    local(K.gain, gain_h, gain)
    local(K.syn, syn_h, syn)

    barrier = pltpu.get_barrier_semaphore()
    friends = peers + [outer, later, before, mate, across]
    for device in friends:
        pl.semaphore_signal(barrier, inc=1, device_id=device, device_id_type=MESH)
    pl.semaphore_wait(barrier, len(friends))

    send(K.g_shift_b, lg_h.at[pl.ds(RG, 128 - RG)], gl.at[rows_b(z, yl, RG)], before)
    send(K.g_shift_a, lg_h.at[pl.ds(0, RG)], gl.at[rows_a(z, yl, RG)], before)

    done = set()
    names = list(steps)
    for name in [names[i] for i in ORDER]:
        copies, after, _, body = steps[name]
        if not done.issuperset(after):
            raise ValueError(name)
        for copy in copies:
            arrive(copy)
        body()
        done.add(name)
    if done != set(steps):
        raise ValueError(sorted(set(steps) - done))

    for name in remote:
        if name not in arrived:
            arrive(name)
        if name not in part_sends:
            remote[name].wait_send()
    for name in local_copies:
        loaded(name)


def tables():
    frequency = ROPE_BASE ** (-(np.arange(HEAD // 2) * 2.0 / HEAD))
    angles = np.arange(LEN)[:, None] * frequency[None, :]
    cosine, sine = np.cos(angles), np.sin(angles)
    return (
        np.concatenate([cosine, cosine], axis=1).astype(np.float32),
        np.concatenate([-sine, sine], axis=1).astype(np.float32),
    )


def emit_kernel(att, grad, att_out, grad_out):
    att_out[...] = att[...]
    grad_out[...] = grad[...]


def on_device(activations, analysis, synthesis, norm_gain, query_weight, keys_values, latent_grad):
    cos, sin = tables()
    anywhere = pl.BlockSpec(memory_space=pl.ANY)

    def vmem(*shape, dtype=BF):
        return pltpu.VMEM(shape, dtype)

    shapes = (jax.ShapeDtypeStruct((LEN, 512), BF), jax.ShapeDtypeStruct((LEN, FEAT), BF))
    attended, grad = pl.pallas_call(
        kernel,
        out_shape=shapes,
        in_specs=[anywhere] * 9,
        out_specs=(anywhere, anywhere),
        scratch_shapes=[
            vmem(LEN, FEAT), vmem(FEAT, LAT), vmem(LAT, FEAT), vmem(1, D, dtype=F32),
            vmem(D, 512), vmem(D, 256), vmem(LEN, HEAD, dtype=F32), vmem(LEN, HEAD, dtype=F32),
            vmem(LEN, LAT), vmem(LEN, LAT), vmem(LEN, LAT), vmem(8, 512, FEAT), vmem(LAT, 768),
            vmem(512, 768, dtype=F32),
            vmem(4, RA, LAT), vmem(2 * RB, HALF), vmem(2 * RB, HALF), vmem(2 * RB, LAT), vmem(2 * RB, LAT),
            vmem(RA, HALF), vmem(RA, HALF), vmem(RA, LAT), vmem(RA, LAT),
            vmem(RB, LAT),
            vmem(8, 1, 128, dtype=F32), vmem(8, 8, 1, 128, dtype=F32),
            pltpu.SemaphoreType.DMA((32,)),
            pltpu.SemaphoreType.DMA((N_COPIES,)),
            pltpu.SemaphoreType.DMA((N_COPIES,)),
        ],
        compiler_params=pltpu.CompilerParams(
            collective_id=0, has_side_effects=True, vmem_limit_bytes=63 * 2**20
        ),
        cost_estimate=pl.CostEstimate(flops=28 * 10**9, bytes_accessed=30 * 10**6, transcendentals=0),
    )(
        activations[0, 0], analysis[0], synthesis[0], norm_gain, query_weight[0], keys_values[0],
        latent_grad[0, 0], jnp.asarray(cos), jnp.asarray(sin),
    )
    attended, grad = pl.pallas_call(
        emit_kernel,
        out_shape=shapes,
        grid=(4,),
        in_specs=[pl.BlockSpec((256, 512), lambda i: (i, 0)), pl.BlockSpec((256, FEAT), lambda i: (i, 0))],
        out_specs=(pl.BlockSpec((256, 512), lambda i: (i, 0)), pl.BlockSpec((256, FEAT), lambda i: (i, 0))),
    )(attended, grad)
    return attended[None, None], grad[None, None]


def solution(mesh):
    return jax.shard_map(
        on_device,
        mesh=mesh,
        in_specs=(
            P("pipe", "dp", None, "tensor"),
            P("pipe", "tensor", None),
            P("pipe", None, "tensor"),
            P("pipe", None),
            P("pipe", None, "tensor"),
            P("pipe", None, "tensor"),
            P("pipe", "dp", "tensor", None),
        ),
        out_specs=(P("pipe", "dp", None, "tensor"), P("pipe", "dp", None, "tensor")),
        check_vma=False,
    )
```

time: 765 us -> 141 us (0.18)
  waiting for transfers between devices: 638 us -> 0 us
  Pallas kernels: 0 us -> 139 us
  matrix products: 57.5 us -> 0 us
  local copies, waits for them, and re-layouts: 24.4 us -> 0 us
  blocking collectives: 17.9 us -> 0 us
  between operations: 14 us -> 0.64 us
  other arithmetic: 9.92 us -> 0 us
    all_gather x3 -> x0, waiting for transfers between devices: 440 us -> none  [the longest x1 318 us: on_device(): portion = lax.all_gather(normed, 'tensor', axis=1, tiled=True)]
    reduce_scatter x1 -> x0, waiting for transfers between devices: 172 us -> none  [on_device(): lax.psum_scatter(jnp.dot(acts_local, w_analysis, preferred_element_type=j...]
    pallas_call x0 -> x2, Pallas kernels: none -> 139 us  [the longest x1 135 us: on_device(): pl.pallas_call(kernel, out_shape=shapes, in_specs=[anywhere] * 9, out_spe...]
    dot_general x9 -> x0, matrix products: 57.5 us -> none  [the longest x1 14.5 us: on_device(): queries_all = jnp.dot(portion, w_query, preferred_element_type=jnp.float32)]
    ppermute x2 -> x0, waiting for transfers between devices: 26.3 us -> none  [passed_along(): return lax.ppermute(value, axis, pairs)]
    psum x1 -> x0, blocking collectives: 17.9 us -> none  [on_device(): squares = lax.psum(jnp.sum(synth_float * synth_float, axis=1), 'tensor')]
    dot_general x1 -> x0, local copies, waits for them, and re-layouts: 11.9 us -> none  [on_device(): queries_all = jnp.dot(portion, w_query, preferred_element_type=jnp.float32)]
  transfers between devices with their start and end apart: 6 -> 0, of which waited for: 6 -> 0; matrix products, arithmetic and copies ran while one was open for 5% -> 0% of each run, Pallas kernels for 0% -> 0%
where the time goes in v2:
time: 141 us; the launch traced here: 140 us
  Pallas kernels  139 us (99%)
    pallas_call x1, Pallas kernels, on_device(): pl.pallas_call(kernel, out_shape=shapes, in_specs=[anywhere] * 9, out_spe...  135 us
    pallas_call x1, Pallas kernels, on_device(): pl.pallas_call(emit_kernel, out_shape=shapes, grid=(4,), in_specs=[pl.Blo...  4.17 us

profile of v2, /device:TPU:6, one launch (start us, length us, event | category | flops | bytes accessed | tf_op | source)
XLA Modules:
  0.0 140.0 jit_solution(12810132135871414090)
XLA Ops:
  0.6 135.2 %shard_map.104 = (bf16[1024,512]{1,0:T(8,128)(2,1)}, bf16[1024,1024]{1,0:T(8,128)(2,1)}) custom-call(bf16[1024,1024]{1,0:T(8,128)(2,1)} %bitcast.12, bf16[1024,2048]{1,0:T(8,128)(2,1)} %bitcast.9, bf16[2048,1024]{1,0:T(8,128)(2,1)} %bitcast.10, f32[1,8192]{1,0:T(1,128)} %gain_h.1, bf16[8192,512]{1,0:T(8,128)(2,1)} %bitcast.8, bf16[8192,256]{1,0:T(8,128)(2,1)} %bitcast.11, ...), custom_call_target="tpu_custom_call" | custom-call | flops 28000000000 | bytes 30000000 | tf_op jit(solution)/shard_map/pallas_call | solution.py:648
  135.8 4.2 %shard_map.105 = (bf16[1024,512]{1,0:T(8,128)(2,1)}, bf16[1024,1024]{1,0:T(8,128)(2,1)}) custom-call(bf16[1024,512]{1,0:T(8,128)(2,1)} %get-tuple-element.6.att, bf16[1024,1024]{1,0:T(8,128)(2,1)} %get-tuple-element.7.grad), custom_call_target="tpu_custom_call" | custom-call | tf_op jit(solution)/shard_map/pallas_call | solution.py:674
